TPU v7x, 32 devices: a whole 2x2x4 slice. The times are simulated.
32 devices in a mesh: seq: 2 (over x), dp: 16 (over z, y, core).
Axes of the slice: x: 2, y: 2, z: 4, core: 2. Of those that a mesh axis runs over, the one named last changes fastest.
Arguments:
- tokens: bfloat16 [16, 1024, 768], P('dp', 'seq'), may hold values from -6 to 6
- cotangent: bfloat16 [16, 1024, 768], P('dp', 'seq'), may hold values from -6 to 6
- attn_weight: bfloat16 [768, 3072], P('dp'), may hold values from -0.21875 to 0.21875
- mlp_weight: bfloat16 [2, 768, 3072], P(None, 'dp'), may hold values from -0.21650635 to 0.21650635
- norms: bfloat16 [4, 768], P(None, 'dp'), may hold values from -1 to 1.5
- taps: bfloat16 [64, 768], P(None, 'dp'), may hold values from -0.375 to 0.375
- ssm_params: float32 [2, 768, 64], P(None, 'seq'), may hold values from -10 to 0.15309311, as said below
- attn_moments: float32 [2, 768, 3072], P(None, 'dp'), may hold values from -1.5 to 2, as said below
- mlp_moments: float32 [2, 2, 768, 3072], P(None, None, 'dp'), may hold values from -1.5 to 2, as said below
- norm_moments: float32 [2, 4, 768], P(None, None, 'dp'), may hold values from -1.5 to 2, as said below
- tap_moments: float32 [2, 64, 768], P(None, None, 'dp'), may hold values from -1.5 to 2, as said below
- ssm_moments: float32 [2, 2, 768, 64], P(None, None, 'seq'), may hold values from -1.5 to 2, as said below
Outputs:
- layer_out: bfloat16 [16, 1024, 768], P('dp', 'seq')
- input_grad: float32 [16, 1024, 768], P('dp', 'seq')
- attn_step: float32 [768, 3072], P('dp')
- attn_moments_new: float32 [2, 768, 3072], P(None, 'dp')
- mlp_step: float32 [2, 768, 3072], P(None, 'dp')
- mlp_moments_new: float32 [2, 2, 768, 3072], P(None, None, 'dp')
- norms_step: float32 [4, 768], P(None, 'dp')
- norm_moments_new: float32 [2, 4, 768], P(None, None, 'dp')
- taps_step: float32 [64, 768], P(None, 'dp')
- tap_moments_new: float32 [2, 64, 768], P(None, None, 'dp')
- ssm_step: float32 [2, 768, 64], P(None, 'seq')
- ssm_moments_new: float32 [2, 2, 768, 64], P(None, None, 'seq')
Inputs may be any that keep to these rules, and one draw needn't show every extreme that they name: ssm_params[0] holds log rates from -10 to -3.5; ssm_params[1] holds coefficients. `attn_moments`: the second moments are positive. `mlp_moments`: the second moments are positive. `norm_moments`: the second moments are positive. `tap_moments`: the second moments are positive. `ssm_moments`: the second moments are positive.
All inputs are finite; a program needn't handle non-finite values.
Results may differ from a plain program's by a relative error of at most 0.01.
Values may be sent and summed in bfloat16 or wider, within the bound.
A program may use at most 320 MiB of HBM per device.

v0:
```python
from functools import partial
import math

import jax
import jax.numpy as jnp
from jax import lax
from jax.sharding import PartitionSpec as P

DFT_ROWS = 256


EPS_NORM = 1e-05
BETA_ONE = 0.9
BETA_TWO = 0.999
ADAM_EPS = 1e-08
LEARN_RATE = 0.001
SSM_LEARN_RATE = 0.00025
DECAY_RATE = 0.1
STEP_COUNT = 10.0
HIGHEST = lax.Precision.HIGHEST


def from_behind(block, axis, distance):
    devices = range(lax.axis_size(axis))
    route = [(i - distance, i) for i in devices if i - distance in devices]
    return lax.ppermute(block, axis, route)


def as_sent(value):

    def short(part):
        return part.astype(jnp.bfloat16) if part.dtype == jnp.float32 else part

    return jax.tree.map(short, value)


def layer_norm(values, gain_row, bias_row):
    average = jnp.mean(values, axis=-1, keepdims=True)
    centred = values - average
    variance = jnp.mean(centred * centred, axis=-1, keepdims=True)
    return centred * lax.rsqrt(variance + EPS_NORM) * gain_row + bias_row


def shift_mix(rim_rows, keys_part, taps_full):
    tap_count = taps_full.shape[0]
    row_count = keys_part.shape[0]
    extended = jnp.concatenate([rim_rows, keys_part], axis=0)
    summed = jnp.zeros_like(keys_part)
    for tap_index in range(tap_count):
        begin_row = tap_count - 1 - tap_index
        summed = summed + taps_full[tap_index] * extended[begin_row : begin_row + row_count]
    return summed


def kernel_rows(length_total, ssm_full):
    inner_count = math.gcd(length_total, 128)
    outer_count = length_total // inner_count
    decay_rates = jnp.exp(ssm_full[0])
    outer_offsets = (jnp.arange(outer_count) * inner_count).astype(jnp.float32)
    inner_offsets = jnp.arange(inner_count).astype(jnp.float32)
    outer_part = ssm_full[1][:, :, None] * jnp.exp(
        -decay_rates[:, :, None] * outer_offsets[None, None, :]
    )
    inner_part = jnp.exp(-decay_rates[:, :, None] * inner_offsets[None, None, :])
    kernel = jnp.einsum("cna,cnb->cab", outer_part, inner_part, precision=HIGHEST)
    return kernel.reshape(kernel.shape[0], length_total)


def dft_tables(length_total, first_count):
    full_length = 2 * length_total
    col_count = full_length // first_count
    half_rows = first_count // 2
    row_index = jnp.arange(half_rows, dtype=jnp.int32)
    freq_index = jnp.arange(first_count, dtype=jnp.int32)
    col_index = jnp.arange(col_count, dtype=jnp.int32)
    angle_first = (
        2.0
        * math.pi
        / first_count
        * (row_index[:, None] * freq_index[None, :] % first_count).astype(jnp.float32)
    )
    angle_twist = (
        2.0 * math.pi / full_length * (freq_index[:, None] * col_index[None, :]).astype(jnp.float32)
    )
    angle_last = (
        2.0
        * math.pi
        / col_count
        * (col_index[:, None] * col_index[None, :] % col_count).astype(jnp.float32)
    )
    return (
        jnp.cos(angle_first),
        jnp.sin(angle_first),
        jnp.cos(angle_twist),
        jnp.sin(angle_twist),
        jnp.cos(angle_last),
        jnp.sin(angle_last),
    )


def forward_dft(signal, tables):
    cos_first, sin_first, cos_twist, sin_twist, cos_last, sin_last = tables
    half_rows = cos_first.shape[0]
    col_count = cos_last.shape[0]
    folded = signal.reshape(signal.shape[0], half_rows, col_count)
    real_first = jnp.einsum("cmp,mk->ckp", folded, cos_first, precision=HIGHEST)
    imaginary_first = -jnp.einsum("cmp,mk->ckp", folded, sin_first, precision=HIGHEST)
    real_twist = real_first * cos_twist + imaginary_first * sin_twist
    imaginary_twist = imaginary_first * cos_twist - real_first * sin_twist
    real_last = jnp.einsum("ckp,pq->ckq", real_twist, cos_last, precision=HIGHEST) + jnp.einsum(
        "ckp,pq->ckq", imaginary_twist, sin_last, precision=HIGHEST
    )
    imaginary_last = jnp.einsum(
        "ckp,pq->ckq", imaginary_twist, cos_last, precision=HIGHEST
    ) - jnp.einsum("ckp,pq->ckq", real_twist, sin_last, precision=HIGHEST)
    return (real_last, imaginary_last)


def inverse_dft(spectrum, tables):
    cos_first, sin_first, cos_twist, sin_twist, cos_last, sin_last = tables
    real_part, imaginary_part = spectrum
    full_length = cos_first.shape[1] * cos_last.shape[0]
    real_inner = jnp.einsum("ckq,qp->ckp", real_part, cos_last, precision=HIGHEST) - jnp.einsum(
        "ckq,qp->ckp", imaginary_part, sin_last, precision=HIGHEST
    )
    imaginary_inner = jnp.einsum(
        "ckq,qp->ckp", imaginary_part, cos_last, precision=HIGHEST
    ) + jnp.einsum("ckq,qp->ckp", real_part, sin_last, precision=HIGHEST)
    real_twist = real_inner * cos_twist - imaginary_inner * sin_twist
    imaginary_twist = imaginary_inner * cos_twist + real_inner * sin_twist
    signal = jnp.einsum("ckp,mk->cmp", real_twist, cos_first, precision=HIGHEST) - jnp.einsum(
        "ckp,mk->cmp", imaginary_twist, sin_first, precision=HIGHEST
    )
    return signal.reshape(signal.shape[0], signal.shape[1] * signal.shape[2]) / full_length


def complex_product(left, right, conjugate_left):
    left_real, left_imaginary = left
    right_real, right_imaginary = right
    if conjugate_left:
        return (
            left_real * right_real + left_imaginary * right_imaginary,
            left_real * right_imaginary - left_imaginary * right_real,
        )
    return (
        left_real * right_real - left_imaginary * right_imaginary,
        left_real * right_imaginary + left_imaginary * right_real,
    )


def adam_update(param_now, moments, gradient, learn_rate, decay_weight):
    first_new = BETA_ONE * moments[0] + (1.0 - BETA_ONE) * gradient
    second_new = BETA_TWO * moments[1] + (1.0 - BETA_TWO) * gradient * gradient
    first_hat = first_new / (1.0 - BETA_ONE**STEP_COUNT)
    second_hat = second_new / (1.0 - BETA_TWO**STEP_COUNT)
    step_size = learn_rate * (
        first_hat / (jnp.sqrt(second_hat) + ADAM_EPS) + decay_weight * param_now
    )
    return (step_size, jnp.stack([first_new, second_new]))


def per_device(
    tokens,
    cotangent,
    attn_weight,
    mlp_weight,
    norms,
    taps,
    ssm_params,
    attn_moments,
    mlp_moments,
    norm_moments,
    tap_moments,
    ssm_moments,
):
    row_count = tokens.shape[1]
    model_width = tokens.shape[2]
    group_count = lax.axis_size("seq")
    owner_count = lax.axis_size("dp")
    length_total = row_count * group_count
    attn_full, mlp_full, norm_full, taps_full = (
        lax.all_gather(attn_weight, "dp", axis=0, tiled=True),
        lax.all_gather(mlp_weight, "dp", axis=1, tiled=True),
        lax.all_gather(norms, "dp", axis=1, tiled=True),
        lax.all_gather(taps, "dp", axis=1, tiled=True),
    )
    inputs = tokens[0].astype(jnp.float32)
    cot_rows = cotangent[0].astype(jnp.float32)
    norm_values = norm_full.astype(jnp.float32)
    taps_values = taps_full.astype(jnp.float32)
    tap_count = taps_values.shape[0]
    normed, norm_pull = jax.vjp(layer_norm, inputs, norm_values[0], norm_values[1])
    normed_low = normed.astype(jnp.bfloat16)
    project = jnp.dot(
        normed_low, attn_full[:, : 3 * model_width], preferred_element_type=jnp.float32
    )
    queries = project[:, :model_width]
    keys_part = project[:, model_width : 2 * model_width]
    values = project[:, 2 * model_width :]
    rim_rows = from_behind(
        keys_part[row_count - tap_count + 1 :].astype(jnp.bfloat16), "seq", 1
    ).astype(jnp.float32)
    shifted, shift_pull = jax.vjp(shift_mix, rim_rows, keys_part, taps_values)
    mixed_rows = (shifted * values).astype(jnp.bfloat16)
    moved_in = lax.all_to_all(mixed_rows.T, "seq", split_axis=0, concat_axis=1, tiled=True).astype(
        jnp.float32
    )
    tables = dft_tables(length_total, DFT_ROWS)
    kernel, kernel_pull = jax.vjp(partial(kernel_rows, length_total), ssm_params)
    kernel_freq = forward_dft(kernel, tables)
    input_freq = forward_dft(moved_in, tables)
    conv_channels = inverse_dft(complex_product(input_freq, kernel_freq, False), tables)
    conv_back = lax.all_to_all(
        conv_channels.astype(jnp.bfloat16), "seq", split_axis=1, concat_axis=0, tiled=True
    )
    conv_rows = conv_back.T.astype(jnp.float32)
    gated_rows = (queries * conv_rows).astype(jnp.bfloat16)
    branch = jnp.dot(
        gated_rows, attn_full[:, 3 * model_width :], preferred_element_type=jnp.float32
    )
    residual_one = inputs + branch
    normed_two, norm_two_pull = jax.vjp(layer_norm, residual_one, norm_values[2], norm_values[3])
    normed_two_low = normed_two.astype(jnp.bfloat16)
    before = jnp.dot(normed_two_low, mlp_full[0], preferred_element_type=jnp.float32)
    active, gelu_pull = jax.vjp(jax.nn.gelu, before)
    active_low = active.astype(jnp.bfloat16)
    mlp_out = jnp.einsum("tf,df->td", active_low, mlp_full[1], preferred_element_type=jnp.float32)
    layer_out = (residual_one + mlp_out).astype(jnp.bfloat16)
    attn_back, mlp_back = (
        lax.all_gather(attn_weight, "dp", axis=0, tiled=True),
        lax.all_gather(mlp_weight, "dp", axis=1, tiled=True),
    )
    grad_after = cotangent[0]
    grad_active = jnp.dot(grad_after, mlp_back[1], preferred_element_type=jnp.float32)
    grad_down = jnp.einsum("td,tf->df", grad_after, active_low, preferred_element_type=jnp.float32)
    grad_before = gelu_pull(grad_active)[0].astype(jnp.bfloat16)
    grad_up = jnp.einsum(
        "td,tf->df", normed_two_low, grad_before, preferred_element_type=jnp.float32
    )
    grad_normed_two = jnp.einsum(
        "tf,df->td", grad_before, mlp_back[0], preferred_element_type=jnp.float32
    )
    grad_residual_part, grad_gain_two, grad_bias_two = norm_two_pull(grad_normed_two)
    grad_residual = cot_rows + grad_residual_part
    grad_branch = grad_residual.astype(jnp.bfloat16)
    grad_out = jnp.einsum("td,te->de", gated_rows, grad_branch, preferred_element_type=jnp.float32)
    grad_gated = jnp.einsum(
        "te,de->td",
        grad_branch,
        attn_back[:, 3 * model_width :],
        preferred_element_type=jnp.float32,
    )
    grad_queries = grad_gated * conv_rows
    grad_conv = (grad_gated * queries).astype(jnp.bfloat16)
    grad_moved = lax.all_to_all(grad_conv.T, "seq", split_axis=0, concat_axis=1, tiled=True).astype(
        jnp.float32
    )
    grad_freq = forward_dft(grad_moved, tables)
    grad_input = inverse_dft(complex_product(kernel_freq, grad_freq, True), tables)
    grad_kernel = inverse_dft(complex_product(input_freq, grad_freq, True), tables)
    grad_ssm_local = kernel_pull(grad_kernel)[0]
    grad_ssm = lax.psum(grad_ssm_local, "dp")
    grad_mixed_back = lax.all_to_all(
        grad_input.astype(jnp.bfloat16), "seq", split_axis=1, concat_axis=0, tiled=True
    )
    grad_mixed = grad_mixed_back.T.astype(jnp.float32)
    grad_shifted = grad_mixed * values
    grad_values = grad_mixed * shifted
    grad_rim, grad_keys, grad_taps = shift_pull(grad_shifted)
    returned = from_behind(as_sent(grad_rim), "seq", -1).astype(grad_rim.dtype)
    grad_keys = grad_keys + jnp.pad(returned, ((row_count - tap_count + 1, 0), (0, 0)))
    grad_project = jnp.concatenate([grad_queries, grad_keys, grad_values], axis=1).astype(
        jnp.bfloat16
    )
    grad_qkv = jnp.einsum("td,te->de", normed_low, grad_project, preferred_element_type=jnp.float32)
    grad_normed = jnp.einsum(
        "te,de->td",
        grad_project,
        attn_back[:, : 3 * model_width],
        preferred_element_type=jnp.float32,
    )
    grad_input_part, grad_gain_one, grad_bias_one = norm_pull(grad_normed)
    input_grad = grad_residual + grad_input_part
    grad_attn = jnp.concatenate([grad_qkv, grad_out], axis=1)
    grad_mlp = jnp.stack([grad_up, grad_down])
    grad_norms = jnp.stack([grad_gain_one, grad_bias_one, grad_gain_two, grad_bias_two])
    owned_part = (
        lax.psum_scatter(
            grad_attn.astype(jnp.bfloat16), "dp", scatter_dimension=0, tiled=True
        ).astype(jnp.float32),
        lax.psum_scatter(
            grad_mlp.astype(jnp.bfloat16), "dp", scatter_dimension=1, tiled=True
        ).astype(jnp.float32),
        lax.psum_scatter(
            grad_norms.astype(jnp.bfloat16), "dp", scatter_dimension=1, tiled=True
        ).astype(jnp.float32),
        lax.psum_scatter(
            grad_taps.astype(jnp.bfloat16), "dp", scatter_dimension=1, tiled=True
        ).astype(jnp.float32),
    )
    summed = (
        lax.psum(owned_part[0].astype(jnp.bfloat16), "seq").astype(jnp.float32),
        lax.psum(owned_part[1].astype(jnp.bfloat16), "seq").astype(jnp.float32),
        lax.psum(owned_part[2].astype(jnp.bfloat16), "seq").astype(jnp.float32),
        lax.psum(owned_part[3].astype(jnp.bfloat16), "seq").astype(jnp.float32),
    )
    grad_scale = 1.0 / math.sqrt(owner_count * length_total)
    attn_step, attn_moments_new = adam_update(
        attn_weight.astype(jnp.float32),
        attn_moments,
        summed[0] * grad_scale,
        LEARN_RATE,
        DECAY_RATE,
    )
    mlp_step, mlp_moments_new = adam_update(
        mlp_weight.astype(jnp.float32), mlp_moments, summed[1] * grad_scale, LEARN_RATE, DECAY_RATE
    )
    norms_step, norm_moments_new = adam_update(
        norms.astype(jnp.float32), norm_moments, summed[2] * grad_scale, LEARN_RATE, 0.0
    )
    taps_step, tap_moments_new = adam_update(
        taps.astype(jnp.float32), tap_moments, summed[3] * grad_scale, LEARN_RATE, DECAY_RATE
    )
    ssm_step, ssm_moments_new = adam_update(
        ssm_params, ssm_moments, grad_ssm * grad_scale, SSM_LEARN_RATE, 0.0
    )
    return (
        layer_out[None],
        input_grad[None],
        attn_step,
        attn_moments_new,
        mlp_step,
        mlp_moments_new,
        norms_step,
        norm_moments_new,
        taps_step,
        tap_moments_new,
        ssm_step,
        ssm_moments_new,
    )


def solution(mesh):
    return jax.shard_map(
        per_device,
        mesh=mesh,
        in_specs=(
            P("dp", "seq", None),
            P("dp", "seq", None),
            P("dp", None),
            P(None, "dp", None),
            P(None, "dp"),
            P(None, "dp"),
            P(None, "seq", None),
            P(None, "dp", None),
            P(None, None, "dp", None),
            P(None, None, "dp"),
            P(None, None, "dp"),
            P(None, None, "seq", None),
        ),
        out_specs=(
            P("dp", "seq", None),
            P("dp", "seq", None),
            P("dp", None),
            P(None, "dp", None),
            P(None, "dp", None),
            P(None, None, "dp", None),
            P(None, "dp"),
            P(None, None, "dp"),
            P(None, "dp"),
            P(None, None, "dp"),
            P(None, "seq", None),
            P(None, None, "seq", None),
        ),
        check_vma=False,
    )
```

profile of v0, /device:TPU:0, one launch (start us, length us, event | category | flops | bytes accessed | tf_op | source)
XLA Modules:
  0.0 869.0 jit_solution(7117007805462785018)
XLA Ops:
  8.7 23.4 %all-gather = bf16[16,48,4]{1,2,0:T(4,128)(2,1)S(1)} all-gather(bf16[1,48,4]{1,2,0:T(4,128)(2,1)} %bitcast.374), channel_id=1, replica_groups=mesh['seq'=2,'dp'=16] {'dp'}, dimensions={0}, use_global_device_ids=true | all-gather | bytes 6528 | tf_op jit(solution)/shard_map/all_gather | solution.py:184
  33.4 18.5 %all_gather.16 = bf16[64,768]{0,1:T(8,128)(2,1)S(1)} all-gather(bf16[64,48]{0,1:T(8,128)(2,1)S(1)} %copy-done.59), channel_id=1, replica_groups=mesh['seq'=2,'dp'=16] {'dp'}, dimensions={1}, use_global_device_ids=true | all-gather | bytes 104448 | tf_op jit(solution)/shard_map/all_gather | solution.py:185
  52.1 11.5 %fusion.1 = f32[384,8,128]{2,1,0:T(8,128)S(1)} fusion(f32[128]{0:T(128)S(1)} %iota_convert_fusion, f32[384,64]{1,0:T(8,128)S(1)} %negate_bitcast_fusion, f32[8]{0:T(128)S(1)} %multiply_convert_fusion.5, f32[384,64]{1,0:T(8,128)S(1)} %copy.169), kind=kOutput, calls=%fused_computation.65 | convolution fusion | flops 305528832 | bytes 1770016 | tf_op jit(solution)/shard_map/jvp(cna,cnb->cab)/dot_general | solution.py:65
  97.9 22.7 %multiply_convert_fusion.4 = (bf16[512,768]{1,0:T(8,128)(2,1)S(1)}, f32[512,768]{1,0:T(8,128)}) fusion(f32[512,2304]{1,0:T(8,128)S(1)} %fusion.33, f32[512,768]{1,0:T(8,128)S(1)} %slice.615, f32[63,768]{1,0:T(8,128)S(1)} %convert_element_type.289, f32[768]{0:T(1024)S(1)} %get-tuple-element.120, f32[768]{0:T(1024)} %get-tuple-element.121, ...), kind=kLoop, calls=%fused_computation.315 | loop fusion | flops 75497472 | bytes 5895168 | tf_op jit(solution)/shard_map/convert_element_type | solution.py:204
  130.4 6.5 all-to-all-done
  139.7 8.1 add_bitcast_fusion.1
  210.3 12.9 %all_to_all.52 = bf16[384,2,512]{0,2,1:T(8,128)(2,1)S(1)} all-to-all(bf16[384,2,512]{0,2,1:T(8,128)(2,1)S(1)} %bitcast.366), channel_id=1, replica_groups=mesh['seq'=2,'dp'=16] {'seq'}, dimensions={1} | all-to-all | bytes 1572864 | tf_op jit(solution)/shard_map/all_to_all | solution.py:213
  298.7 11.3 %multiply_subtract_fusion.1 = (f32[384,256,8]{1,2,0:T(8,128)}, f32[384,256,8]{1,2,0:T(8,128)S(1)}, f32[384,256,8]{1,2,0:T(8,128)S(1)}, f32[384,256,8]{1,2,0:T(8,128)S(1)}) fusion(f32[384,256,8]{1,2,0:T(8,128)} %get-tuple-element.306, f32[384,256,8]{1,2,0:T(8,128)S(1)} %convolution_add_fusion.5, f32[384,256,8]{1,2,0:T(8,128)} %convolution_subtract_fusion.2, ...), kind=kOutput, calls=%fused_computation.107 | convolution fusion | flops 85721984 | bytes 34603008 | tf_op jit(solution)/shard_map/ckp,pq->ckq/dot_general | solution.py:110
  353.1 28.7 %multiply_reduce_fusion = f32[384,64]{1,0:T(8,128)} fusion(f32[128]{0:T(128)} %copy-done.180, f32[384,64]{1,0:T(8,128)S(1)} %copy-done.55, f32[384,8,128]{2,1,0:T(8,128)} %copy.208, f32[8]{0:T(128)S(1)} %copy-done.179, f32[384,64]{1,0:T(8,128)S(1)} %copy-done.53), kind=kOutput, calls=%fused_computation.62 | convolution fusion | flops 314941440 | bytes 1868320 | tf_op jit(solution)/shard_map/transpose(jvp(cna,cnb->cab))/dot_general | solution.py:65
  396.0 20.9 %multiply_reduce_fusion.2 = (f32[384,64]{1,0:T(8,128)S(1)}, f32[384,64]{1,0:T(8,128)S(1)}) fusion(f32[8]{0:T(128)S(1)} %copy-done.179, f32[384,64]{1,0:T(8,128)S(1)} %copy-done.55, f32[384,64]{1,0:T(8,128)S(1)} %copy-done.53, f32[384,8,128]{2,1,0:T(8,128)S(1)} %copy-done.40, f32[128]{0:T(128)} %copy-done.180), kind=kOutput, calls=%fused_computation.237 | convolution fusion | flops 306462720 | bytes 1966624 | tf_op jit(solution)/shard_map/transpose(jvp(cna,cnb->cab))/dot_general | solution.py:65
  423.5 6.8 broadcast_multiply_fusion.2
  430.5 7.1 multiply_reduce_fusion.3
  437.8 10.3 %broadcast_multiply_fusion.1 = (f32[512,768]{1,0:T(8,128)}, f32[512,768]{1,0:T(8,128)}, f32[512,768]{1,0:T(8,128)}, f32[512,768]{1,0:T(8,128)}, f32[512,768]{1,0...) fusion(f32[512,768]{1,0:T(8,128)S(1)} %get-tuple-element.191, ...), kind=kLoop, calls=%fused_computation.345 | loop fusion | flops 7077888 | bytes 29939712 | tf_op jit(solution)/shard_map/transpose(jvp())/mul | solution.py:51
  448.3 9.6 %broadcast_multiply_fusion = (f32[512,768]{1,0:T(8,128)}, f32[512,768]{1,0:T(8,128)}, f32[512,768]{1,0:T(8,128)}, f32[512,768]{1,0:T(8,128)}, f32[512,768]{1,0:T...) fusion(f32[512,768]{1,0:T(8,128)S(1)} %get-tuple-element.191, ...), kind=kLoop, calls=%fused_computation.344 | loop fusion | flops 7077888 | bytes 29939712 | tf_op jit(solution)/shard_map/transpose(jvp())/mul | solution.py:51
  457.9 31.0 %pad_add_fusion = f32[575,768]{1,0:T(8,128)S(1)} fusion(f32[512,768]{1,0:T(8,128)S(1)} %get-tuple-element.220, f32[512,768]{1,0:T(8,128)S(1)} %get-tuple-element.221, f32[512,768]{1,0:T(8,128)S(1)} %get-tuple-element.222, f32[512,768]{1,0:T(8,128)S(1)} %get-tuple-element.223, f32[512,768]{1,0:T(8,128)S(1)} %get-tuple-element.224, ...), kind=kLoop, calls=%fused_computation.153 | loop fusion | flops 27820800 | bytes 102429696 | tf_op jit(solution)/shard_map/transpose(jvp())/add_any | solution.py:51
  501.7 7.5 fusion.13
  509.2 7.9 fusion.14
  517.1 8.9 %pad_maximum_fusion = bf16[2,768,3072]{2,1,0:T(8,128)(2,1)} fusion(bf16[1,768,3072]{2,1,0:T(8,128)(2,1)} %fusion.14, bf16[1,768,3072]{2,1,0:T(8,128)(2,1)} %fusion.13), kind=kLoop, calls=%fused_computation.66 | loop fusion | flops 4718592 | bytes 18874368 | tf_op jit(solution)/shard_map/stack | solution.py:285
  535.3 9.3 %fusion.123 = bf16[1,512,768]{2,1,0:T(8,128)(2,1)} fusion(f32[512,768]{1,0:T(8,128)} %copy-done.29, bf16[2,768,3072]{2,1,0:T(8,128)(2,1)} %all-gather.6.cloned.1.call-done, f32[512,3072]{1,0:T(8,128)} %copy-done.181), kind=kOutput, calls=%fused_computation.318 | convolution fusion | flops 2430861312 | bytes 13369344 | tf_op jit(solution)/shard_map/tf,df->td/dot_general | solution.py:227
  587.6 113.4 %reduce-scatter.11.cloned.1.call-done = bf16[2,48,3072]{2,1,0:T(8,128)(2,1)} async-done(((bf16[2,768,3072]{2,1,0:T(8,128)(2,1)}), bf16[2,48,3072]{2,1,0:T(8,128)(2,1)}) %reduce-scatter.11.cloned.1.call-update) | async-done | bytes 589840 | tf_op jit(solution)/shard_map/reduce_scatter | solution.py:291
  704.4 54.4 %reduce-scatter.13.cloned.1.call-done = bf16[48,4]{1,0:T(8,128)(2,1)} async-done(((bf16[768,4]{1,0:T(8,128)(2,1)}), bf16[48,4]{1,0:T(8,128)(2,1)}) %reduce-scatter.13.cloned.1.call-update) | async-done | bytes 400
  759.5 56.3 %reduce-scatter.15.cloned.1.call-done = bf16[48,64]{1,0:T(8,128)(2,1)} async-done(((bf16[768,64]{1,0:T(8,128)(2,1)}), bf16[48,64]{1,0:T(8,128)(2,1)}) %reduce-scatter.15.cloned.1.call-update) | async-done | bytes 6160
  816.6 8.3 all-reduce.131
  828.4 25.6 %all-reduce.138.cloned.1.call-done = (bf16[48,3072]{1,0:T(8,128)(2,1)}, bf16[2,48,3072]{2,1,0:T(8,128)(2,1)}) async-done(((bf16[48,3072]{1,0:T(8,128)(2,1)}, bf16[2,48,3072]{2,1,0:T(8,128)(2,1)}), (bf16[48,3072]{1,0:T(8,128)(2,1)}, bf16[2,48,3072]{2,1,0:T(8,128)(2,1)})) %all-reduce.138.cloned.1.call-update) | async-done | bytes 884752 | tf_op jit(solution)/shard_map/psum | solution.py:302
  (600 shorter events, 330.4 us)
Async XLA Ops:
  7.2 26.1 %copy-start.51 = (f32[2,384,64]{1,2,0:T(8,128)S(1)}, f32[2,384,64]{1,2,0:T(8,128)}, u32[]{:S(2)}) copy-start(f32[2,384,64]{1,2,0:T(8,128)} %param.18) | copy-start | bytes 589828
  7.2 26.2 %copy-start.59 = (bf16[64,48]{0,1:T(8,128)(2,1)S(1)}, bf16[64,48]{0,1:T(8,128)(2,1)}, u32[]{:S(2)}) copy-start(bf16[64,48]{0,1:T(8,128)(2,1)} %param.17) | copy-start | bytes 18436
  7.2 80.1 %all-gather.4.cloned.1.call-start = ((), (), s32[]{:S(2)}) async-start(), calls=%async_computation.8 | async-start | bytes 5013504 | tf_op jit(solution)/shard_map/all_gather | solution.py:182
  7.9 221.6 %all-gather.6.cloned.1.call-start = ((), (), s32[]{:S(2)}) async-start(), calls=%async_computation.9 | async-start | bytes 10027008 | tf_op jit(solution)/shard_map/all_gather | solution.py:183
  33.3 30.4 %copy-start.32 = (f32[2,384,64]{2,1,0:T(8,128)}, f32[2,384,64]{2,1,0:T(8,128)S(1)}, u32[]{:S(2)}) copy-start(f32[2,384,64]{2,1,0:T(8,128)S(1)} %copy.170) | copy-start | bytes 589828
  33.4 30.2 %copy-start.52 = (f32[384,64]{1,0:T(8,128)}, f32[384,64]{1,0:T(8,128)S(1)}, u32[]{:S(2)}) copy-start(f32[384,64]{1,0:T(8,128)S(1)} %copy.169) | copy-start | bytes 294916
  91.6 5.9 collective-permute-start
  121.6 15.3 %all-to-all-start = ((bf16[2,384,512]{1,2,0:T(8,128)(2,1)}), bf16[2,384,512]{1,2,0:T(8,128)(2,1)S(1)}, u32[]{:S(2)}, u32[]{:S(2)}) async-start(bf16[2,384,512]{1,2,0:T(8,128)(2,1)} %bitcast.356), calls=%async_computation | async-start | bytes 1572864 | tf_op jit(solution)/shard_map/all_to_all | solution.py:205
  252.6 13.8 %all-to-all-start.2 = ((bf16[2,384,512]{1,2,0:T(8,128)(2,1)}), bf16[2,384,512]{1,2,0:T(8,128)(2,1)}, u32[]{:S(2)}, u32[]{:S(2)}) async-start(bf16[2,384,512]{1,2,0:T(8,128)(2,1)} %bitcast.365), calls=%async_computation.2 | async-start | bytes 1572864 | tf_op jit(solution)/shard_map/all_to_all | solution.py:255
  392.0 25.9 %all-to-all-start.3 = ((bf16[384,2,512]{0,2,1:T(8,128)(2,1)}), bf16[384,2,512]{0,2,1:T(8,128)(2,1)S(1)}, u32[]{:S(2)}, u32[]{:S(2)}) async-start(bf16[384,2,512]{0,2,1:T(8,128)(2,1)} %bitcast.40), calls=%async_computation.3 | async-start | bytes 1572864 | tf_op jit(solution)/shard_map/all_to_all | solution.py:263
  395.6 149.1 %all-reduce.136.cloned.1.call-start = ((), (), s32[]{:S(2)}) async-start(), calls=%async_computation.12 | async-start | bytes 786432 | tf_op jit(solution)/shard_map/psum | solution.py:262
  417.8 169.8 %reduce-scatter.9.cloned.1.call-start = ((), (), s32[]{:S(2)}) async-start(), calls=%async_computation.10 | async-start | bytes 5013504 | tf_op jit(solution)/shard_map/reduce_scatter | solution.py:288
  488.9 6.5 collective-permute-start.1
  501.6 199.4 %reduce-scatter.11.cloned.1.call-start = ((), (), s32[]{:S(2)}) async-start(), calls=%async_computation.11 | async-start | bytes 10027008 | tf_op jit(solution)/shard_map/reduce_scatter | solution.py:291
  526.1 232.6 %reduce-scatter.13.cloned.1.call-start = ((), (), s32[]{:S(2)}) async-start(), calls=%async_computation.13 | async-start | bytes 208896
  582.9 118.2 %copy-start.26 = (bf16[1,512,768]{2,1,0:T(8,128)(2,1)S(1)}, bf16[1,512,768]{2,1,0:T(8,128)(2,1)}, u32[]{:S(2)}) copy-start(bf16[1,512,768]{2,1,0:T(8,128)(2,1)} %param.12) | copy-start | bytes 2359300
  582.9 118.2 %copy-start.36 = (bf16[1,512,768]{2,1,0:T(8,128)(2,1)S(1)}, bf16[1,512,768]{2,1,0:T(8,128)(2,1)}, u32[]{:S(2)}) copy-start(bf16[1,512,768]{2,1,0:T(8,128)(2,1)} %param.13) | copy-start | bytes 2359300
  584.3 116.7 %copy-start.19 = (f32[512,768]{1,0:T(8,128)S(1)}, f32[512,768]{1,0:T(8,128)}, u32[]{:S(2)}) copy-start(f32[512,768]{1,0:T(8,128)} %copy-done.18) | copy-start | bytes 4718596
  584.3 116.7 %copy-start.144 = (f32[512]{0:T(512)S(1)}, f32[512]{0:T(512)}, u32[]{:S(2)}) copy-start(f32[512]{0:T(512)} %copy-done.143) | copy-start | bytes 6148
  585.3 230.6 %reduce-scatter.15.cloned.1.call-start = ((), (), s32[]{:S(2)}) async-start(), calls=%async_computation.14 | async-start | bytes 208896
  586.9 267.1 %all-reduce.138.cloned.1.call-start = ((), (), s32[]{:S(2)}) async-start(), calls=%async_computation.15 | async-start | bytes 1769472 | tf_op jit(solution)/shard_map/psum | solution.py:302
  701.0 123.9 %copy-start.57 = (f32[1,64,48]{2,1,0:T(8,128)S(1)}, f32[1,64,48]{2,1,0:T(8,128)}, u32[]{:S(2)}) copy-start(f32[1,64,48]{2,1,0:T(8,128)} %copy.235) | copy-start | bytes 36868
  701.1 123.9 %copy-start.58 = (f32[1,64,48]{2,1,0:T(8,128)S(1)}, f32[1,64,48]{2,1,0:T(8,128)}, u32[]{:S(2)}) copy-start(f32[1,64,48]{2,1,0:T(8,128)} %copy.234) | copy-start | bytes 36868
  701.1 152.9 %copy-start.42 = (bf16[48,3072]{1,0:T(8,128)(2,1)S(1)}, bf16[48,3072]{1,0:T(8,128)(2,1)}, u32[]{:S(2)}) copy-start(bf16[48,3072]{1,0:T(8,128)(2,1)} %param.14) | copy-start | bytes 884740
  (172 other events, 1554.1 us)
Sparse Core Ops, SparseCore 0:
  10.3 56.7 all-gather.3
  69.4 80.3 all-gather.5
  417.9 89.8 all-reduce.135
  512.0 74.5 reduce-scatter.8
  590.6 110.3 reduce-scatter.10
  705.3 53.3 reduce-scatter.12
  763.2 52.5 reduce-scatter.14
  818.3 35.6 all-reduce.137
where the time goes:
time: 880 us; the launch traced here: 869 us
  matrix products  271 us (31%)
  waiting for transfers between devices  267 us (30%)
  other arithmetic  144 us (16%)
  local copies, waits for them, and re-layouts  88.3 us (10%)
  blocking collectives  63.1 us (7%)
  starting transfers between devices  18 us (2%)
  between operations  17.6 us (2%)
    reduce_scatter x1, waiting for transfers between devices, per_device(): lax.psum_scatter(grad_mlp.astype(jnp.bfloat16), 'dp', scatter_dimension=1...  113 us
    unnamed x10, waiting for transfers between devices  112 us
    dot_general x3, matrix products, kernel_rows(): jnp.einsum('cna,cnb->cab', outer_part, inner_part, precision=HIGHEST)  61.1 us
    add_any x1, other arithmetic, shift_mix(): extended[begin_row:begin_row + row_count]  31 us
    mul x3, other arithmetic, shift_mix(): taps_full[tap_index] * extended[begin_row:begin_row + row_count]  26.7 us
    reduce_sum x8, other arithmetic, shift_mix(): taps_full[tap_index] * extended[begin_row:begin_row + row_count]  26.2 us
    psum x1, waiting for transfers between devices, per_device(): lax.psum(owned_part[0].astype(jnp.bfloat16), 'seq').astype(jnp.float32)  25.6 us
    all_gather x1, blocking collectives, per_device(): lax.all_gather(norms, 'dp', axis=1, tiled=True)  23.4 us
  transfers between devices with their start and end apart: 13, of which 8 were waited for; matrix products, arithmetic and copies ran while one was open for 39% of the time, Pallas kernels for 0%

commit v1 on v0

--- a/solution.py
+++ b/solution.py
@@ -3,7 +3,11 @@
 
 import jax
 import jax.numpy as jnp
+import ml_dtypes
+import numpy as np
 from jax import lax
+from jax.experimental import pallas as pl
+from jax.experimental.pallas import tpu as pltpu
 from jax.sharding import PartitionSpec as P
 
 DFT_ROWS = 256
@@ -340,9 +344,852 @@
     )
 
 
+LANES = 128
+RADIX = 8
+HALF = 128
+
+
+def transform_tables():
+    rows = np.arange(HALF)
+    length = RADIX * HALF
+    waves = RADIX * rows[None, :, None] + np.arange(RADIX)[:, None, None] + 0.25
+    angles = 2.0 * np.pi * np.mod(rows[None, None, :] * waves, length) / length
+    cosines, sines = np.cos(angles), np.sin(angles)
+    full = np.concatenate(
+        [np.concatenate([cosines, sines], axis=2), np.concatenate([-sines, cosines], axis=2)], axis=1
+    )
+
+    def parts(matrix):
+        matrix = matrix.astype(np.float32)
+        high = matrix.astype(ml_dtypes.bfloat16)
+        rest = (matrix - high.astype(np.float32)).astype(ml_dtypes.bfloat16)
+        return np.stack([high, rest])
+
+    return parts(full), parts(np.swapaxes(full, 1, 2))
+
+
+def turned(value, angle):
+    real, imaginary = value
+    cosine, sine = math.cos(angle), math.sin(angle)
+    if abs(sine) < 1e-12:
+        return (real, imaginary) if cosine > 0 else (-real, -imaginary)
+    if abs(cosine) < 1e-12:
+        return (-imaginary, real) if sine > 0 else (imaginary, -real)
+    return (real * cosine - imaginary * sine, real * sine + imaginary * cosine)
+
+
+def small_transform(values, sign):
+    count = len(values)
+    if count == 1:
+        return values
+    even = small_transform(values[::2], sign)
+    odd = small_transform(values[1::2], sign)
+    low, high = [], []
+    for index in range(count // 2):
+        (er, ei), (tr, ti) = even[index], turned(odd[index], sign * 2.0 * math.pi * index / count)
+        low.append((er + tr, ei + ti))
+        high.append((er - tr, ei - ti))
+    return low + high
+
+
+def split(value):
+    high = value.astype(jnp.bfloat16)
+    return high, (value - high.astype(jnp.float32)).astype(jnp.bfloat16)
+
+
+def dot(left, right):
+    return jnp.dot(left, right, preferred_element_type=jnp.float32)
+
+
+def each_tile(width, rows, step, body):
+    for block in range(width // LANES):
+
+        def one(index, carry, block=block):
+            body(pl.multiple_of(index * step, step), pl.ds(block * LANES, LANES))
+            return carry
+
+        lax.fori_loop(0, rows // step, one, 0)
+
+
+def to_waves(width, read, used, w_ref, high_ref, low_ref, store):
+    def first(row, cols):
+        inputs = []
+        for part in range(used):
+            x = read(part * HALF, row, cols)
+            angle = -2.0 * math.pi * part / 32.0
+            inputs.append((x * math.cos(angle), x * math.sin(angle)) if part else (x, jnp.zeros_like(x)))
+        while len(inputs) < RADIX:
+            inputs.append((jnp.zeros_like(x), jnp.zeros_like(x)))
+        for wave, value in enumerate(small_transform(inputs, -1.0)):
+            for place, part in enumerate(value):
+                high, low = split(part)
+                high_ref[wave, pl.ds(row + place * HALF, 16), cols] = high
+                low_ref[wave, pl.ds(row + place * HALF, 16), cols] = low
+
+    each_tile(width, HALF, 16, first)
+
+    def second(wave, carry):
+        high = high_ref[wave]
+        store(wave, dot(w_ref[0, wave], high) + dot(w_ref[1, wave], high) + dot(w_ref[0, wave], low_ref[wave]))
+        return carry
+
+    lax.fori_loop(0, RADIX, second, 0)
+
+
+def product(width, left_ref, right_ref, conjugate, high_ref, low_ref):
+    sign = -1.0 if conjugate else 1.0
+
+    def one(wave, carry):
+        def tile(row, cols):
+            lr, li = left_ref[wave, pl.ds(row, 16), cols], left_ref[wave, pl.ds(row + HALF, 16), cols] * sign
+            rr, ri = right_ref[wave, pl.ds(row, 16), cols], right_ref[wave, pl.ds(row + HALF, 16), cols]
+            for place, part in enumerate((lr * rr - li * ri, lr * ri + li * rr)):
+                high, low = split(part)
+                high_ref[wave, pl.ds(row + place * HALF, 16), cols] = high
+                low_ref[wave, pl.ds(row + place * HALF, 16), cols] = low
+
+        each_tile(width, HALF, 16, tile)
+        return carry
+
+    lax.fori_loop(0, RADIX, one, 0)
+
+
+def from_waves(width, w_ref, high_ref, low_ref, back_ref, put):
+    def second(wave, carry):
+        high = high_ref[wave]
+        back_ref[wave] = dot(w_ref[0, wave], high) + dot(w_ref[1, wave], high) + dot(w_ref[0, wave], low_ref[wave])
+        return carry
+
+    lax.fori_loop(0, RADIX, second, 0)
+    scale = 1.0 / (RADIX * HALF)
+
+    def first(row, cols):
+        values = [
+            (back_ref[wave, pl.ds(row, 16), cols], back_ref[wave, pl.ds(row + HALF, 16), cols])
+            for wave in range(RADIX)
+        ]
+        for part, (real, imaginary) in enumerate(small_transform(values, 1.0)):
+            angle = 2.0 * math.pi * part / 32.0
+            put(part * HALF, row, cols, real * (math.cos(angle) * scale) - imaginary * (math.sin(angle) * scale))
+
+    each_tile(width, HALF, 16, first)
+
+
+def first_positions(width, count, w_ref, high_ref, low_ref):
+    total = jnp.zeros((count, width), jnp.float32)
+    for wave in range(RADIX):
+        wh, wl = w_ref[0, wave, :count, :], w_ref[1, wave, :count, :]
+        high = high_ref[wave]
+        total = total + (dot(wh, high) + dot(wl, high) + dot(wh, low_ref[wave]))
+    return total * (1.0 / (RADIX * HALF))
+
+
+FINE = 32
+
+
+def decay_sums(width, length, ssm_ref, coarse_ref, fine_ref, out_ref):
+    modes = ssm_ref.shape[1]
+    steps = length // FINE
+    offsets = lax.broadcasted_iota(jnp.int32, (FINE, width), 0).astype(jnp.float32)
+    starts = lax.broadcasted_iota(jnp.int32, (steps, width), 0).astype(jnp.float32) * FINE
+
+    def powers(index, carry):
+        base = pl.multiple_of(index * 8, 8)
+        rates = jnp.exp(ssm_ref[0, pl.ds(base, 8), :])
+        weights = ssm_ref[1, pl.ds(base, 8), :]
+        for i in range(8):
+            fine_ref[base + i] = jnp.exp(-rates[i : i + 1] * offsets)
+            coarse_ref[base + i] = weights[i : i + 1] * jnp.exp(-rates[i : i + 1] * starts)
+        return carry
+
+    lax.fori_loop(0, modes // 8, powers, 0)
+    for block in range(width // LANES):
+        cols = pl.ds(block * LANES, LANES)
+
+        def group(index, carry, cols=cols):
+            def add(mode, sums):
+                fine = fine_ref[mode, :, cols]
+                rows = coarse_ref[mode, pl.ds(pl.multiple_of(index * 8, 8), 8), cols]
+                return tuple(s + rows[i : i + 1] * fine for i, s in enumerate(sums))
+
+            sums = lax.fori_loop(0, modes, add, tuple(jnp.zeros((FINE, LANES), jnp.float32) for _ in range(8)))
+            for i, s in enumerate(sums):
+                out_ref[pl.ds(pl.multiple_of(index * 8 * FINE, FINE) + i * FINE, FINE), cols] = s
+            return carry
+
+        lax.fori_loop(0, steps // 8, group, 0)
+
+
+def decay_gradients(width, length, ssm_ref, grad_ref, out_ref):
+    modes = ssm_ref.shape[1]
+    steps = length // FINE
+    for block in range(width // LANES):
+        cols = pl.ds(block * LANES, LANES)
+        offsets = lax.broadcasted_iota(jnp.int32, (FINE, LANES), 0).astype(jnp.float32)
+
+        def group(index, carry, cols=cols, offsets=offsets):
+            base = pl.multiple_of(index * 8, 8)
+            rates = jnp.exp(ssm_ref[0, pl.ds(base, 8), cols])
+            leaps = jnp.exp(-rates * FINE)
+            plain_rows, slope_rows = [], []
+            for modes_now in ((0, 1, 2, 3), (4, 5, 6, 7)):
+                zero = offsets * 0.0
+                leap_rows = [leaps[i : i + 1] for i in modes_now]
+
+                def step(number, sums, leap_rows=leap_rows):
+                    rows = grad_ref[pl.ds(pl.multiple_of((steps - 1 - number) * FINE, FINE), FINE), cols]
+                    return tuple((v * leap + rows, w * leap + v) for (v, w), leap in zip(sums, leap_rows))
+
+                sums = lax.fori_loop(0, steps, step, tuple((zero, zero) for _ in modes_now))
+                for i, (v, w) in zip(modes_now, sums):
+                    fine = jnp.exp(-rates[i : i + 1] * offsets)
+                    plain = fine * v
+                    slope = fine * w * (leaps[i : i + 1] * FINE) + plain * offsets
+                    plain_rows.append(jnp.sum(plain, axis=0, keepdims=True))
+                    slope_rows.append(jnp.sum(slope, axis=0, keepdims=True))
+            out_ref[1, pl.ds(base, 8), cols] = jnp.concatenate(plain_rows, axis=0)
+            out_ref[0, pl.ds(base, 8), cols] = (
+                -ssm_ref[1, pl.ds(base, 8), cols] * rates * jnp.concatenate(slope_rows, axis=0)
+            )
+            return carry
+
+        lax.fori_loop(0, modes // 8, group, 0)
+
+
+def mixer_forward_body(
+    proj_ref, taps_ref, ssm_ref, to_ref, from_ref,
+    gated_ref, conv_ref, shifted_ref, kernel_w, taps_w, keys_w, mixed_w,
+    line_ref, high_ref, low_ref, back_ref, coarse_ref, fine_ref,
+):
+    width = conv_ref.shape[1]
+    length = conv_ref.shape[0]
+
+    def keep(target):
+        def store(wave, value):
+            target[wave] = value
+
+        return store
+
+    def lines(base, row, cols):
+        return line_ref[pl.ds(base + row, 16), cols]
+
+    def column(place, cols):
+        return pl.ds(place * width + cols.start, cols.size)
+
+    decay_sums(width, length, ssm_ref, coarse_ref, fine_ref, line_ref)
+    to_waves(width, lines, RADIX, to_ref, high_ref, low_ref, keep(kernel_w))
+    to_waves(
+        width, lambda base, row, cols: taps_ref[pl.ds(base + row, 16), cols],
+        1, to_ref, high_ref, low_ref, keep(taps_w),
+    )
+    to_waves(
+        width, lambda base, row, cols: proj_ref[pl.ds(base + row, 16), column(1, cols)],
+        RADIX, to_ref, high_ref, low_ref, keep(keys_w),
+    )
+    product(width, taps_w, keys_w, False, high_ref, low_ref)
+
+    def put_shifted(base, row, cols, value):
+        rows = pl.ds(base + row, 16)
+        shifted_ref[rows, cols] = value
+        mixed = value * proj_ref[rows, column(2, cols)]
+        line_ref[rows, cols] = mixed.astype(jnp.bfloat16).astype(jnp.float32)
+
+    from_waves(width, from_ref, high_ref, low_ref, back_ref, put_shifted)
+    to_waves(width, lines, RADIX, to_ref, high_ref, low_ref, keep(mixed_w))
+    product(width, kernel_w, mixed_w, False, high_ref, low_ref)
+
+    def put_conv(base, row, cols, value):
+        rows = pl.ds(base + row, 16)
+        rounded = value.astype(jnp.bfloat16)
+        conv_ref[rows, cols] = rounded
+        gated_ref[rows, cols] = (proj_ref[rows, cols] * rounded.astype(jnp.float32)).astype(jnp.bfloat16)
+
+    from_waves(width, from_ref, high_ref, low_ref, back_ref, put_conv)
+
+
+def mixer_backward_body(
+    grad_ref, proj_ref, conv_ref, shifted_ref, kernel_w, taps_w, keys_w, mixed_w, ssm_ref, to_ref, from_ref,
+    out_ref, taps_out_ref, ssm_out_ref,
+    line_ref, decay_ref, wave_ref, high_ref, low_ref, back_ref,
+):
+    width = conv_ref.shape[1]
+    length = conv_ref.shape[0]
+
+    def keep(wave, value):
+        wave_ref[wave] = value
+
+    def lines(base, row, cols):
+        return line_ref[pl.ds(base + row, 16), cols]
+
+    def column(place, cols):
+        return pl.ds(place * width + cols.start, cols.size)
+
+    def read_conv_grad(base, row, cols):
+        rows = pl.ds(base + row, 16)
+        gradient = grad_ref[rows, cols].astype(jnp.float32)
+        out_ref[rows, cols] = (gradient * conv_ref[rows, cols].astype(jnp.float32)).astype(jnp.bfloat16)
+        return (gradient * proj_ref[rows, cols]).astype(jnp.bfloat16).astype(jnp.float32)
+
+    to_waves(width, read_conv_grad, RADIX, to_ref, high_ref, low_ref, keep)
+    product(width, kernel_w, wave_ref, True, high_ref, low_ref)
+
+    def put_mixed(base, row, cols, value):
+        rows = pl.ds(base + row, 16)
+        gradient = value.astype(jnp.bfloat16).astype(jnp.float32)
+        out_ref[rows, column(2, cols)] = (gradient * shifted_ref[rows, cols]).astype(jnp.bfloat16)
+        line_ref[rows, cols] = gradient * proj_ref[rows, column(2, cols)]
+
+    from_waves(width, from_ref, high_ref, low_ref, back_ref, put_mixed)
+    product(width, mixed_w, wave_ref, True, high_ref, low_ref)
+
+    def put_kernel(base, row, cols, value):
+        decay_ref[pl.ds(base + row, 16), cols] = value
+
+    from_waves(width, from_ref, high_ref, low_ref, back_ref, put_kernel)
+    to_waves(width, lines, RADIX, to_ref, high_ref, low_ref, keep)
+    product(width, taps_w, wave_ref, True, high_ref, low_ref)
+
+    def put_keys(base, row, cols, value):
+        out_ref[pl.ds(base + row, 16), column(1, cols)] = value.astype(jnp.bfloat16)
+
+    from_waves(width, from_ref, high_ref, low_ref, back_ref, put_keys)
+    product(width, keys_w, wave_ref, True, high_ref, low_ref)
+    taps_out_ref[...] = first_positions(width, taps_out_ref.shape[0], from_ref, high_ref, low_ref)
+    decay_gradients(width, length, ssm_ref, decay_ref, ssm_out_ref)
+
+
+VMEM_LIMIT = 58 * 1024 * 1024
+
+
+def mixer_forward(proj, taps, ssm, to_table, from_table):
+    length, width = proj.shape[0], proj.shape[1] // 3
+    modes = ssm.shape[1]
+    f32, low = jnp.float32, jnp.bfloat16
+    waves = (RADIX, 2 * HALF, width)
+    vmem = pl.BlockSpec(memory_space=pltpu.VMEM)
+    return pl.pallas_call(
+        mixer_forward_body,
+        out_shape=(
+            jax.ShapeDtypeStruct((length, width), low),
+            jax.ShapeDtypeStruct((length, width), low),
+            jax.ShapeDtypeStruct((length, width), f32),
+        )
+        + (jax.ShapeDtypeStruct(waves, f32),) * 4,
+        in_specs=[vmem] * 5,
+        out_specs=(vmem,) * 7,
+        scratch_shapes=[
+            pltpu.VMEM((length, width), f32),
+            pltpu.VMEM(waves, low),
+            pltpu.VMEM(waves, low),
+            pltpu.VMEM(waves, f32),
+            pltpu.VMEM((modes, length // FINE, width), f32),
+            pltpu.VMEM((modes, FINE, width), f32),
+        ],
+        compiler_params=pltpu.CompilerParams(vmem_limit_bytes=VMEM_LIMIT),
+        name="mixer_forward",
+    )(proj, taps, ssm, to_table, from_table)
+
+
+def mixer_backward(grad, proj, conv, shifted, kernel_w, taps_w, keys_w, mixed_w, ssm, to_table, from_table, tap_count):
+    length, width = conv.shape
+    f32, low = jnp.float32, jnp.bfloat16
+    waves = (RADIX, 2 * HALF, width)
+    vmem = pl.BlockSpec(memory_space=pltpu.VMEM)
+    return pl.pallas_call(
+        mixer_backward_body,
+        out_shape=(
+            jax.ShapeDtypeStruct((length, 3 * width), low),
+            jax.ShapeDtypeStruct((tap_count, width), f32),
+            jax.ShapeDtypeStruct(ssm.shape, f32),
+        ),
+        in_specs=[vmem] * 11,
+        out_specs=(vmem,) * 3,
+        scratch_shapes=[
+            pltpu.VMEM((length, width), f32),
+            pltpu.VMEM((length, width), f32),
+            pltpu.VMEM(waves, f32),
+            pltpu.VMEM(waves, low),
+            pltpu.VMEM(waves, low),
+            pltpu.VMEM(waves, f32),
+        ],
+        compiler_params=pltpu.CompilerParams(vmem_limit_bytes=VMEM_LIMIT),
+        name="mixer_backward",
+    )(grad, proj, conv, shifted, kernel_w, taps_w, keys_w, mixed_w, ssm, to_table, from_table)
+
+
+MESH = pl.DeviceIdType.MESH
+TWO, FOUR = 2, 4
+
+
+class Place:
+    def __init__(self):
+        self.s, self.d = lax.axis_index("seq"), lax.axis_index("dp")
+        self.z, self.y, self.c = self.d // 4, (self.d // 2) % 2, self.d % 2
+
+    def over_x(self):
+        return (1 - self.s, self.d)
+
+    def over_y(self):
+        return (self.s, self.d + 2 - 4 * self.y)
+
+    def over_core(self):
+        return (self.s, self.d + 1 - 2 * self.c)
+
+    def along_z(self, step):
+        return (self.s, (self.d + 4 * step) % 16)
+
+    def owner(self, index):
+        return (self.s, index)
+
+
+def send(source, target, send_sem, recv_sem, device):
+    return pltpu.make_async_remote_copy(
+        src_ref=source, dst_ref=target, send_sem=send_sem, recv_sem=recv_sem, device_id=device, device_id_type=MESH
+    )
+
+
+def greet_all(place):
+    barrier = pltpu.get_barrier_semaphore()
+    pl.semaphore_signal(barrier, inc=1, device_id=place.over_x(), device_id_type=MESH)
+
+    def greet(step, carry):
+        pl.semaphore_signal(
+            barrier, inc=1, device_id=place.owner((place.d + step) % 16), device_id_type=MESH
+        )
+        return carry
+
+    lax.fori_loop(1, 16, greet, 0)
+    pl.semaphore_wait(barrier, 16)
+
+
+def add_blocks(target, sources, count):
+    def one(index, carry):
+        total = sources[0](index).astype(jnp.float32)
+        for source in sources[1:]:
+            total = total + source(index).astype(jnp.float32)
+        target(index, total)
+        return carry
+
+    lax.fori_loop(0, count, one, 0)
+
+
+PIECES = (
+    (0, 0, 1536, "whole"),
+    (1, 0, 1536, "halved"),
+    (0, 1536, 1536, "whole"),
+    (1, 1536, 1536, "halved"),
+    (3, 0, 1152, "apart"),
+    (2, 0, 768, "halved"),
+)
+
+
+def reduce_body(*refs):
+    count = len(PIECES)
+    grads, refs = refs[:4], refs[4:]
+    (small_ref, ssm_ref), refs = refs[:2], refs[2:]
+    outs, refs = refs[:count], refs[count:]
+    (small_out, ssm_out), refs = refs[:2], refs[2:]
+    near, mine, from_x, from_y, from_z, final, last = (refs[i * count : (i + 1) * count] for i in range(7))
+    refs = refs[7 * count :]
+    small_all, small_sum, small_last, ssm_all, ssm_sum = refs[:5]
+    (own_sem, core_s, core_r, x_s, x_r, y_s, y_r, z_s, z_r, f_s, f_r, sm_s, sm_r, ss_s, ss_r, sg_s, sg_r, last_sem) = refs[5:]
+    place = Place()
+    greet_all(place)
+
+    def core_copy(k, h):
+        source, start, width, way = PIECES[k]
+        part = width // TWO if way == "halved" else width
+        columns = grads[source].at[:, :, 1 - place.c, :, pl.ds(start + h * part, part)]
+        return send(columns, near[k].at[h], core_s.at[k, h], core_r.at[k, h], place.over_core())
+
+    def own_copy(k, h):
+        source, start, width, way = PIECES[k]
+        part = width // TWO if way == "halved" else width
+        columns = grads[source].at[:, :, place.c, :, pl.ds(start + h * part, part)]
+        return pltpu.make_async_copy(columns, mine[k].at[h], own_sem.at[k, h])
+
+    def halves(k):
+        return range(TWO if PIECES[k][3] == "halved" else 1)
+
+    for k in range(count):
+        for h in halves(k):
+            core_copy(k, h).start()
+            own_copy(k, h).start()
+
+    def to_peer(source, target, send_sem, recv_sem, step):
+        other = (place.d + step) % 16
+        return send(source.at[other], target.at[place.d], send_sem.at[other], recv_sem.at[place.d], place.owner(other))
+
+    def from_peer(target, send_sem, recv_sem, step):
+        other = (place.d + step) % 16
+        return send(target.at[other], target.at[other], send_sem.at[other], recv_sem.at[other], place.owner(other))
+
+    def share(step):
+        other = (place.d + step) % 16
+        return send(
+            ssm_sum.at[place.d], ssm_sum.at[place.d], sg_s.at[other], sg_r.at[place.d], place.owner(other)
+        )
+
+    def over_peers(action):
+        def one(step, carry):
+            action(step)
+            return carry
+
+        lax.fori_loop(1, 16, one, 0)
+
+    over_peers(lambda step: to_peer(small_ref, small_all, sm_s, sm_r, step).start())
+    over_peers(lambda step: to_peer(ssm_ref, ssm_all, ss_s, ss_r, step).start())
+
+    def x_copy(k):
+        return send(mine[k].at[1 - place.s], from_x[k], x_s.at[k], x_r.at[k], place.over_x())
+
+    def kept(k):
+        return mine[k].at[place.s] if PIECES[k][3] == "halved" else mine[k].at[0]
+
+    def y_copy(k):
+        return send(kept(k).at[:, 1 - place.y], from_y[k], y_s.at[k], y_r.at[k], place.over_y())
+
+    def z_copy(k, step):
+        other = (place.z + step) % 4
+        return send(
+            kept(k).at[other, place.y], from_z[k].at[step - 1], z_s.at[k, step - 1], z_r.at[k, step - 1],
+            place.along_z(step),
+        )
+
+    def last_copy(k):
+        return send(final[k], last[k], f_s.at[k], f_r.at[k], place.over_x())
+
+    def add_core(k):
+        for h in halves(k):
+            core_copy(k, h).wait_recv()
+            own_copy(k, h).wait()
+
+            def put(index, total, h=h):
+                mine[k][h, index // 2, index % 2] = total.astype(jnp.bfloat16)
+
+            add_blocks(
+                put,
+                [lambda i, h=h: mine[k][h, i // 2, i % 2], lambda i, h=h: near[k][h, i // 2, i % 2]],
+                8,
+            )
+        if PIECES[k][3] == "halved":
+            x_copy(k).start()
+        else:
+            y_copy(k).start()
+
+    def add_x(k):
+        x_copy(k).wait_recv()
+
+        def put(index, total):
+            kept(k)[index // 2, index % 2] = total.astype(jnp.bfloat16)
+
+        add_blocks(
+            put, [lambda i: kept(k)[i // 2, i % 2], lambda i: from_x[k][i // 2, i % 2]], 8
+        )
+        y_copy(k).start()
+
+    def add_y(k):
+        y_copy(k).wait_recv()
+
+        def put(index, total):
+            kept(k)[index, place.y] = total.astype(jnp.bfloat16)
+
+        add_blocks(put, [lambda i: kept(k)[i, place.y], lambda i: from_y[k][i]], 4)
+        for step in range(1, 4):
+            z_copy(k, step).start()
+
+    def add_z(k):
+        for step in range(1, 4):
+            z_copy(k, step).wait_recv()
+        total = kept(k)[place.z, place.y].astype(jnp.float32)
+        for step in range(3):
+            total = total + from_z[k][step].astype(jnp.float32)
+        final[k][...] = total.astype(jnp.bfloat16)
+        last_copy(k).start()
+
+    def finish(k):
+        last_copy(k).wait_recv()
+        if PIECES[k][3] == "whole":
+            outs[k][...] = (final[k][...].astype(jnp.float32) + last[k][...].astype(jnp.float32)).astype(
+                outs[k].dtype
+            )
+        else:
+            outs[k][place.s] = final[k][...]
+            outs[k][1 - place.s] = last[k][...]
+
+    for k in range(count):
+        add_core(k)
+
+    over_peers(lambda step: from_peer(ssm_all, ss_s, ss_r, step).wait_recv())
+    ssm_all[place.d] = ssm_ref[place.d]
+    total = ssm_all[0]
+    for index in range(1, 16):
+        total = total + ssm_all[index]
+    ssm_sum[place.d] = total
+    over_peers(lambda step: share(step).start())
+
+    over_peers(lambda step: from_peer(small_all, sm_s, sm_r, step).wait_recv())
+    total = small_ref[place.d].astype(jnp.float32)
+
+    def add_small(step, total):
+        return total + small_all[(place.d + step) % 16].astype(jnp.float32)
+
+    small_sum[...] = lax.fori_loop(1, 16, add_small, total).astype(jnp.bfloat16)
+    small_final = send(small_sum, small_last, last_sem.at[0], last_sem.at[1], place.over_x())
+    small_final.start()
+
+    order = [k for k in range(count) if PIECES[k][3] != "halved"]
+    crossed = [k for k in range(count) if PIECES[k][3] == "halved"]
+    for i in range(max(len(order), len(crossed))):
+        if i < len(order):
+            add_y(order[i])
+        if i < len(crossed):
+            add_x(crossed[i])
+    for i in range(max(len(order), len(crossed))):
+        if i < len(crossed):
+            add_y(crossed[i])
+        if i < len(order):
+            add_z(order[i])
+    for k in crossed:
+        add_z(k)
+    over_peers(lambda step: from_peer(ssm_sum, sg_s, sg_r, step).wait_recv())
+    ssm_out[...] = ssm_sum[...]
+    small_final.wait_recv()
+    small_out[...] = small_sum[...].astype(jnp.float32) + small_last[...].astype(jnp.float32)
+    for k in order + crossed:
+        finish(k)
+
+    for k in range(count):
+        for h in halves(k):
+            core_copy(k, h).wait_send()
+        if PIECES[k][3] == "halved":
+            x_copy(k).wait_send()
+        y_copy(k).wait_send()
+        for step in range(1, 4):
+            z_copy(k, step).wait_send()
+        last_copy(k).wait_send()
+    small_final.wait_send()
+    over_peers(lambda step: to_peer(small_ref, small_all, sm_s, sm_r, step).wait_send())
+    over_peers(lambda step: to_peer(ssm_ref, ssm_all, ss_s, ss_r, step).wait_send())
+    over_peers(lambda step: share(step).wait_send())
+
+
+def reduce_gradients(down, up, out, qkv, small, ssm):
+    f32, low = jnp.float32, jnp.bfloat16
+    count = len(PIECES)
+    owned = down.shape[3]
+    vmem, anywhere = pl.BlockSpec(memory_space=pltpu.VMEM), pl.BlockSpec(memory_space=pl.ANY)
+    results, near, mine, from_x, from_y, from_z, final, last = [], [], [], [], [], [], [], []
+    for _, _, width, way in PIECES:
+        halves = TWO if way == "halved" else 1
+        part = width // halves
+        results.append(jax.ShapeDtypeStruct((owned, part) if way == "whole" else (TWO, owned, part), f32 if way == "whole" else low))
+        near.append(pltpu.VMEM((halves, FOUR, TWO, owned, part), low))
+        mine.append(pltpu.VMEM((halves, FOUR, TWO, owned, part), low))
+        from_x.append(pltpu.VMEM((FOUR, TWO, owned, part) if way == "halved" else (1, 1, 16, LANES), low))
+        from_y.append(pltpu.VMEM((FOUR, owned, part), low))
+        from_z.append(pltpu.VMEM((3, owned, part), low))
+        final.append(pltpu.VMEM((owned, part), low))
+        last.append(pltpu.VMEM((owned, part), low))
+    dma = pltpu.SemaphoreType.DMA
+    results += [jax.ShapeDtypeStruct(small.shape[1:], f32), jax.ShapeDtypeStruct(ssm.shape, f32)]
+    return pl.pallas_call(
+        reduce_body,
+        out_shape=tuple(results),
+        in_specs=[anywhere] * 4 + [vmem] * 2,
+        out_specs=(vmem,) * (count + 2),
+        scratch_shapes=near
+        + mine
+        + from_x
+        + from_y
+        + from_z
+        + final
+        + last
+        + [
+            pltpu.VMEM(small.shape, low),
+            pltpu.VMEM(small.shape[1:], low),
+            pltpu.VMEM(small.shape[1:], low),
+            pltpu.VMEM(ssm.shape, f32),
+            pltpu.VMEM(ssm.shape, f32),
+            dma((count, TWO)),
+            dma((count, TWO)),
+            dma((count, TWO)),
+            dma((count,)),
+            dma((count,)),
+            dma((count,)),
+            dma((count,)),
+            dma((count, 3)),
+            dma((count, 3)),
+            dma((count,)),
+            dma((count,)),
+            dma((16,)),
+            dma((16,)),
+            dma((16,)),
+            dma((16,)),
+            dma((16,)),
+            dma((16,)),
+            dma((2,)),
+        ],
+        compiler_params=pltpu.CompilerParams(
+            collective_id=1, has_side_effects=True, vmem_limit_bytes=VMEM_LIMIT
+        ),
+        name="reduce_gradients",
+    )(down, up, out, qkv, small, ssm)
+
+
+def layer_norm_parts(values):
+    average = jnp.mean(values, axis=-1, keepdims=True)
+    centred = values - average
+    variance = jnp.mean(centred * centred, axis=-1, keepdims=True)
+    inverse = lax.rsqrt(variance + EPS_NORM)
+    return centred * inverse, inverse
+
+
+def layer_norm_back(upstream, normal, inverse, gain_row):
+    weighted = upstream * gain_row
+    average = jnp.mean(weighted, axis=-1, keepdims=True)
+    overlap = jnp.mean(weighted * normal, axis=-1, keepdims=True)
+    into = (weighted - average - normal * overlap) * inverse
+    return into, jnp.sum(upstream * normal, axis=0), jnp.sum(upstream, axis=0)
+
+
+def per_device_split(
+    tokens,
+    cotangent,
+    attn_weight,
+    mlp_weight,
+    norms,
+    taps,
+    ssm_params,
+    attn_moments,
+    mlp_moments,
+    norm_moments,
+    tap_moments,
+    ssm_moments,
+):
+    f32, low = jnp.float32, jnp.bfloat16
+    rows, width = tokens.shape[1:]
+    shares = lax.axis_size("seq")
+    owners = lax.axis_size("dp")
+    length = rows * shares
+    part = width // shares
+    half = lax.axis_index("seq")
+    tap_count = taps.shape[0]
+    to_table, from_table = map(jnp.asarray, transform_tables())
+
+    owned = attn_weight.shape[0]
+    columns = lax.dynamic_index_in_dim(attn_weight.reshape(owned, 4, shares, part), half, 2, False)
+    qkv_shard = columns[:, :3].reshape(owned, 3 * part)
+    small = lax.all_gather(jnp.concatenate([norms, taps]), "dp", axis=1, tiled=True).astype(f32)
+    token_all = lax.all_gather(tokens[0], "seq", axis=0, tiled=True)
+    qkv_full = lax.all_gather(qkv_shard, "dp", axis=0, tiled=True)
+    out_full = lax.all_gather(attn_weight[:, 3 * width :], "dp", axis=0, tiled=True)
+    mlp_full = lax.all_gather(mlp_weight, "dp", axis=1, tiled=True)
+    norm_rows, tap_rows = small[:4], small[4:]
+    tap_part = lax.dynamic_slice_in_dim(tap_rows, half * part, part, 1)
+    ssm_turned = jnp.swapaxes(ssm_params, 1, 2)
+
+    normal_all, inverse_all = layer_norm_parts(token_all.astype(f32))
+    normed_low = (normal_all * norm_rows[0] + norm_rows[1]).astype(low)
+    proj = dot(normed_low, qkv_full)
+    gated, conv, shifted, kernel_w, taps_w, keys_w, mixed_w = mixer_forward(
+        proj, jnp.pad(tap_part, ((0, HALF - tap_count), (0, 0))), ssm_turned, to_table, from_table
+    )
+    gated_rows = lax.all_to_all(gated, "seq", split_axis=0, concat_axis=1, tiled=True)
+    inputs = tokens[0].astype(f32)
+    residual = inputs + dot(gated_rows, out_full)
+    normal_two, inverse_two = layer_norm_parts(residual)
+    normed_two = (normal_two * norm_rows[2] + norm_rows[3]).astype(low)
+    before = dot(normed_two, mlp_full[0])
+    active, gelu_pull = jax.vjp(jax.nn.gelu, before)
+    active_low = active.astype(low)
+    grad_after = cotangent[0]
+    layer_out = (
+        residual + jnp.einsum("tf,df->td", active_low, mlp_full[1], preferred_element_type=f32)
+    ).astype(low)
+    grad_active = dot(grad_after, mlp_full[1])
+    grad_down = jnp.einsum("td,tf->df", grad_after, active_low, preferred_element_type=f32)
+    grad_before = gelu_pull(grad_active)[0].astype(low)
+    grad_up = jnp.einsum("td,tf->df", normed_two, grad_before, preferred_element_type=f32)
+    grad_normed_two = jnp.einsum("tf,df->td", grad_before, mlp_full[0], preferred_element_type=f32)
+    into_two, gain_two, bias_two = layer_norm_back(grad_normed_two, normal_two, inverse_two, norm_rows[2])
+    grad_residual = grad_after.astype(f32) + into_two
+    grad_branch = grad_residual.astype(low)
+    grad_out = jnp.einsum("td,te->de", gated_rows, grad_branch, preferred_element_type=f32)
+    grad_gated = jnp.einsum("te,de->td", grad_branch, out_full, preferred_element_type=f32).astype(low)
+    grad_gated_part = lax.all_to_all(grad_gated, "seq", split_axis=1, concat_axis=0, tiled=True)
+    grad_proj, grad_taps, grad_ssm = mixer_backward(
+        grad_gated_part, proj, conv, shifted, kernel_w, taps_w, keys_w, mixed_w,
+        ssm_turned, to_table, from_table, tap_count,
+    )
+    grad_qkv = jnp.einsum("td,te->de", normed_low, grad_proj, preferred_element_type=f32)
+    grad_normed = jnp.einsum("te,de->td", grad_proj, qkv_full, preferred_element_type=f32)
+    grad_normed_rows = lax.psum_scatter(
+        grad_normed.astype(low), "seq", scatter_dimension=0, tiled=True
+    ).astype(f32)
+    normal_one, inverse_one = layer_norm_parts(inputs)
+    into_one, gain_one, bias_one = layer_norm_back(grad_normed_rows, normal_one, inverse_one, norm_rows[0])
+    input_grad = grad_residual + into_one
+
+    def by_owner(gradient):
+        return gradient.astype(low).reshape(FOUR, TWO, TWO, owned, gradient.shape[1])
+
+    scale = 1.0 / math.sqrt(owners * length)
+    norm_part = jnp.stack([gain_one, bias_one, gain_two, bias_two])
+    tap_spread = lax.dynamic_update_slice(jnp.zeros((tap_count, width), f32), grad_taps, (0, half * part))
+    small_part = jnp.concatenate([norm_part, tap_spread, jnp.zeros((LANES - 4 - tap_count, width), f32)])
+    sums = reduce_gradients(
+        by_owner(grad_down),
+        by_owner(grad_up),
+        by_owner(grad_out),
+        by_owner(grad_qkv),
+        small_part.astype(low).T.reshape(owners, owned, LANES),
+        grad_ssm.reshape(owners, -1, part),
+    )
+    down_sum = jnp.concatenate([sums[0], sums[2]], axis=1)
+    up_sum = jnp.concatenate([sums[1][0], sums[1][1], sums[3][0], sums[3][1]], axis=1).astype(f32)
+    qkv_sum = jnp.swapaxes(sums[4].reshape(shares, owned, 3, part), 0, 1).swapaxes(1, 2)
+    attn_sum = jnp.concatenate(
+        [qkv_sum.reshape(owned, 3 * width), sums[5][0], sums[5][1]], axis=1
+    )
+    mlp_sum = jnp.stack([up_sum, down_sum])
+    small_sum = sums[6].T[: 4 + tap_count]
+    ssm_sum = jnp.swapaxes(sums[7].reshape(ssm_turned.shape), 1, 2)
+
+    attn_step, attn_new = adam_update(
+        attn_weight.astype(f32), attn_moments, attn_sum.astype(f32) * scale, LEARN_RATE, DECAY_RATE
+    )
+    mlp_step, mlp_new = adam_update(
+        mlp_weight.astype(f32), mlp_moments, mlp_sum.astype(f32) * scale, LEARN_RATE, DECAY_RATE
+    )
+    norms_step, norm_new = adam_update(norms.astype(f32), norm_moments, small_sum[:4] * scale, LEARN_RATE, 0.0)
+    taps_step, tap_new = adam_update(taps.astype(f32), tap_moments, small_sum[4:] * scale, LEARN_RATE, DECAY_RATE)
+    ssm_step, ssm_new = adam_update(ssm_params, ssm_moments, ssm_sum * scale, SSM_LEARN_RATE, 0.0)
+    return (
+        layer_out[None],
+        input_grad[None],
+        attn_step,
+        attn_new,
+        mlp_step,
+        mlp_new,
+        norms_step,
+        norm_new,
+        taps_step,
+        tap_new,
+        ssm_step,
+        ssm_new,
+    )
+
+
 def solution(mesh):
+    fits = (mesh.shape["seq"], mesh.shape["dp"]) == (2, 16)
+
+    def chosen(tokens, *others):
+        plan = per_device_split if fits and tokens.shape[1] * 2 == RADIX * HALF else per_device
+        return plan(tokens, *others)
+
     return jax.shard_map(
-        per_device,
+        chosen,
         mesh=mesh,
         in_specs=(
             P("dp", "seq", None),

time: 880 us -> 494 us (0.56)
  matrix products: 271 us -> 57.9 us
  Pallas kernels: 0 us -> 213 us
  waiting for transfers between devices: 267 us -> 106 us
  other arithmetic: 144 us -> 28.4 us
  local copies, waits for them, and re-layouts: 88.3 us -> 36.6 us
  blocking collectives: 63.1 us -> 23.6 us
  starting transfers between devices: 18 us -> 7.44 us
    dot_general x51 -> x12, matrix products: 271 us -> 57.9 us  [the longest x4 19.6 us: dot(): return jnp.dot(left, right, preferred_element_type=jnp.float32)]
    pallas_call x0 -> x3, Pallas kernels: none -> 213 us  [the longest x1 82.6 us: reduce_gradients(): pl.pallas_call(reduce_body, out_shape=tuple(results), in_specs=[anywhere]...]
    reduce_scatter x2 -> x1, waiting for transfers between devices: 113 us -> 0.01 us  [per_device_split(): lax.psum_scatter(grad_normed.astype(low), 'seq', scatter_dimension=0, til...]
    unnamed x10 -> x5, waiting for transfers between devices: 112 us -> 1.25 us
    all_gather x2 -> x4, waiting for transfers between devices: 0.02 us -> 83.7 us  [the longest x1 40.8 us: per_device_split(): mlp_full = lax.all_gather(mlp_weight, 'dp', axis=1, tiled=True)]
    add_any x2 -> x0, other arithmetic: 31.7 us -> none  [the longest x1 31 us: shift_mix(): extended[begin_row:begin_row + row_count]]
    psum x2 -> x0, waiting for transfers between devices: 25.6 us -> none  [the longest x1 25.6 us: per_device(): lax.psum(owned_part[0].astype(jnp.bfloat16), 'seq').astype(jnp.float32)]
    convert_element_type x9 -> x1, other arithmetic: 25.6 us -> 0.02 us  [per_device_split(): lax.all_gather(jnp.concatenate([norms, taps]), 'dp', axis=1, tiled=True)]
  transfers between devices with their start and end apart: 13 -> 7, of which waited for: 8 -> 5; matrix products, arithmetic and copies ran while one was open for 39% -> 10% of each run, Pallas kernels for 0% -> 11%
where the time goes in v1:
time: 494 us; the launch traced here: 487 us
  Pallas kernels  213 us (43%)
  waiting for transfers between devices  106 us (21%)
  matrix products  57.9 us (12%)
  local copies, waits for them, and re-layouts  36.6 us (7%)
  other arithmetic  28.4 us (6%)
  blocking collectives  23.6 us (5%)
  between operations  14.9 us (3%)
  starting transfers between devices  7.44 us (2%)
    pallas_call x1, Pallas kernels, reduce_gradients(): pl.pallas_call(reduce_body, out_shape=tuple(results), in_specs=[anywhere]...  82.6 us
    pallas_call x1, Pallas kernels, mixer_backward(): pl.pallas_call(mixer_backward_body, out_shape=(jax.ShapeDtypeStruct((leng...  74.7 us
    pallas_call x1, Pallas kernels, mixer_forward(): pl.pallas_call(mixer_forward_body, out_shape=(jax.ShapeDtypeStruct((lengt...  55.4 us
    all_gather x1, waiting for transfers between devices, per_device_split(): mlp_full = lax.all_gather(mlp_weight, 'dp', axis=1, tiled=True)  40.8 us
    all_gather x1, waiting for transfers between devices, per_device_split(): qkv_full = lax.all_gather(qkv_shard, 'dp', axis=0, tiled=True)  40.6 us
    all_gather x1, blocking collectives, per_device_split(): lax.all_gather(jnp.concatenate([norms, taps]), 'dp', axis=1, tiled=True)  23.6 us
    dot_general x4, matrix products, dot(): return jnp.dot(left, right, preferred_element_type=jnp.float32)  19.6 us
    all_to_all x1, waiting for transfers between devices, per_device_split(): lax.all_to_all(grad_gated, 'seq', split_axis=1, concat_axis=0, tiled=True)  11 us
  transfers between devices with their start and end apart: 7, of which 5 were waited for; matrix products, arithmetic and copies ran while one was open for 10% of the time, Pallas kernels for 11%

profile of v1, /device:TPU:0, one launch (start us, length us, event | category | flops | bytes accessed | tf_op | source)
XLA Modules:
  0.0 487.4 jit_solution(12685645320791084620)
XLA Ops:
  12.6 23.6 %all_gather.16 = bf16[68,768]{0,1:T(8,128)(2,1)S(1)} all-gather(bf16[68,48]{0,1:T(8,128)(2,1)S(1)} %pad_maximum_fusion.7), channel_id=1, replica_groups=mesh['seq'=2,'dp'=16] {'dp'}, dimensions={1}, use_global_device_ids=true | all-gather | bytes 110976 | tf_op jit(solution)/shard_map/all_gather | solution.py:1083
  37.2 2.3 all-gather.12.cloned.1.call-done
  42.0 40.6 %all-gather.6.cloned.1.call-done = bf16[768,1152]{1,0:T(8,128)(2,1)} async-done(((bf16[48,1152]{1,0:T(8,128)(2,1)}), bf16[768,1152]{1,0:T(8,128)(2,1)}) %all-gather.6.cloned.1.call-update) | async-done | bytes 1769488 | tf_op jit(solution)/shard_map/all_gather | solution.py:1085
  82.6 6.0 %fusion.66.proj_ref = f32[1024,1152]{1,0:T(8,128)} fusion(bf16[768,1152]{1,0:T(8,128)(2,1)} %all-gather.6.cloned.1.call-done, bf16[1,1024,768]{2,1,0:T(8,128)(2,1)S(1)} %copy-done.3, f32[768]{0:T(1024)S(1)} %get-tuple-element.117, f32[768]{0:T(1024)S(1)} %get-tuple-element.118, f32[1024]{0:T(1024)S(1)} %add_rsqrt_fusion, f32[1024]{0:T(1024)S(1)} %broadcast_multiply_fusion.3), kind=kOutput, calls=%fused_computation.152 | convolution fusion | flops 1816657920 | bytes 8075264 | tf_op jit(solution)/shard_map/dot_general | solution.py:401
  88.7 55.4 %mixer_forward.1 = (bf16[1024,384]{1,0:T(8,128)(2,1)}, bf16[1024,384]{1,0:T(8,128)(2,1)}, f32[1024,384]{1,0:T(8,128)}, f32[8,256,384]{2,1,0:T(8,128)}, f32[8,256...) custom-call(f32[1024,1152]{1,0:T(8,128)} %fusion.66.proj_ref, f32[128,384]{1,0:T(8,128)} %pad.4.taps_ref, ...), custom_call_target="tpu_custom_call" | custom-call | tf_op jit(solution)/shard_map/mixer_forward/pallas_call | solution.py:670
  144.1 2.4 copy.102
  146.4 3.7 all-to-all-start
  151.8 9.8 %all-to-all-done = bf16[2,512,384]{1,2,0:T(8,128)(2,1)S(1)} async-done(((bf16[2,512,384]{1,2,0:T(8,128)(2,1)}), bf16[2,512,384]{1,2,0:T(8,128)(2,1)S(1)}, u32[]{:S(2)}, u32[]{:S(2)}) %all-to-all-start) | async-done | bytes 786464 | tf_op jit(solution)/shard_map/all_to_all | solution.py:1098
  161.6 2.4 fusion.72
  164.4 40.8 %all-gather.10.cloned.1.call-done = bf16[2,768,3072]{2,1,0:T(8,128)(2,1)} async-done(((bf16[2,48,3072]{2,1,0:T(8,128)(2,1)}), bf16[2,768,3072]{2,1,0:T(8,128)(2,1)}) %all-gather.10.cloned.1.call-update) | async-done | bytes 9437200 | tf_op jit(solution)/shard_map/all_gather | solution.py:1087
  205.1 4.8 fusion.8
  210.5 6.3 %fusion.6 = bf16[512,3072]{1,0:T(8,128)(2,1)S(1)} fusion(f32[512,3072]{1,0:T(8,128)S(1)} %fusion.8, bf16[2,768,3072]{2,1,0:T(8,128)(2,1)S(1)} %copy-done.45, bf16[1,512,768]{2,1,0:T(8,128)(2,1)S(1)} %copy-done.16), kind=kOutput, calls=%fused_computation.8 | convolution fusion | flops 2447376384 | bytes 14942208 | tf_op jit(solution)/shard_map/dot_general | solution.py:401
  216.8 3.5 multiply_reduce_fusion
  224.2 3.5 all-to-all-start.1
  228.2 11.0 %all-to-all-done.1 = bf16[512,2,384]{2,0,1:T(8,128)(2,1)S(1)} async-done(((bf16[512,2,384]{2,0,1:T(8,128)(2,1)}), bf16[512,2,384]{2,0,1:T(8,128)(2,1)S(1)}, u32[]{:S(2)}, u32[]{:S(2)}) %all-to-all-start.1) | async-done | bytes 786464 | tf_op jit(solution)/shard_map/all_to_all | solution.py:1120
  240.1 74.7 %mixer_backward.1 = (bf16[1024,1152]{1,0:T(8,128)(2,1)}, f32[64,384]{1,0:T(8,128)}, f32[2,64,384]{2,1,0:T(8,128)}) custom-call(bf16[1024,384]{1,0:T(8,128)(2,1)} %bitcast.205, f32[1024,1152]{1,0:T(8,128)} %fusion.66.proj_ref, bf16[1024,384]{1,0:T(8,128)(2,1)} %get-tuple-element.31.conv_ref, f32[1024,384]{1,0:T(8,128)} %get-tuple-element.32.shifted_ref, ...), custom_call_target="tpu_custom_call" | custom-call | tf_op jit(solution)/shard_map/mixer_backward/pallas_call | solution.py:698
  314.9 5.0 %convolution_convert_fusion.3 = bf16[1024,768]{1,0:T(8,128)(2,1)} fusion(bf16[1024,1152]{1,0:T(8,128)(2,1)} %get-tuple-element.37, bf16[768,1152]{1,0:T(8,128)(2,1)S(1)} %copy-done.46), kind=kOutput, calls=%fused_computation.41 | convolution fusion | flops 1812725760 | bytes 5701632 | tf_op jit(solution)/shard_map/te,de->td/dot_general | solution.py:1126
  319.9 7.4 %convolution_convert_fusion = bf16[768,3072]{1,0:T(8,128)(2,1)} fusion(bf16[512,3072]{1,0:T(8,128)(2,1)} %copy-done.49, f32[512,768]{1,0:T(8,128)} %copy-done.4, f32[768]{0:T(1024)S(1)} %get-tuple-element.116, f32[768]{0:T(1024)S(1)} %get-tuple-element.115, f32[512]{0:T(512)S(1)} %add_rsqrt_fusion.2, f32[512]{0:T(512)S(1)} %broadcast_multiply_fusion.9), kind=kOutput, calls=%fused_computation.10 | convolution fusion | flops 2420244480 | bytes 9447424 | tf_op jit(solution)/shard_map/td,tf->df/dot_general | solution.py:1113
  329.6 8.8 %convolution_convert_fusion.1 = bf16[3072,768]{0,1:T(8,128)(2,1)} fusion(bf16[1,512,768]{2,1,0:T(8,128)(2,1)S(1)} %copy-done.17, f32[512,3072]{1,0:T(8,128)} %copy-done.48), kind=kOutput, calls=%fused_computation.11 | convolution fusion | flops 2432434176 | bytes 11796480 | tf_op jit(solution)/shard_map/td,tf->df/dot_general | solution.py:1111
  338.5 4.7 fusion.33
  344.7 6.2 %convolution_convert_fusion.2 = bf16[768,1152]{1,0:T(8,128)(2,1)} fusion(bf16[1024,1152]{1,0:T(8,128)(2,1)} %get-tuple-element.37, bf16[1,1024,768]{2,1,0:T(8,128)(2,1)} %all-gather.12.cloned.1.call-done, f32[768]{0:T(1024)S(1)} %copy-done.39, f32[768]{0:T(1024)S(1)} %get-tuple-element.118, f32[1024]{0:T(1024)S(1)} %copy-done.42, f32[1024]{0:T(1024)S(1)} %copy-done.31), kind=kOutput, calls=%fused_computation.20 | convolution fusion | flops 1817542656 | bytes 5715968 | tf_op jit(solution)/shard_map/td,te->de/dot_general | solution.py:1125
  350.9 2.6 fusion.32
  356.1 2.1 concatenate.71
  358.2 82.6 %reduce_gradients.1 = (f32[48,1536]{1,0:T(8,128)}, bf16[2,48,768]{2,1,0:T(8,128)(2,1)}, f32[48,1536]{1,0:T(8,128)}, bf16[2,48,768]{2,1,0:T(8,128)(2,1)}, bf16[2,...) custom-call(bf16[4,2,2,48,3072]{4,3,2,1,0:T(8,128)(2,1)} %bitcast.202, ...), custom_call_target="tpu_custom_call" | custom-call | tf_op jit(solution)/shard_map/reduce_gradients/pallas_call | solution.py:996
  (200 shorter events, 62.0 us)
Async XLA Ops:
  7.2 32.3 %all-gather.12.cloned.1.call-start = ((), (), s32[]{:S(2)}) async-start(), calls=%async_computation.7 | async-start | bytes 2359296 | tf_op jit(solution)/shard_map/all_gather | solution.py:1084
  7.9 74.7 %all-gather.6.cloned.1.call-start = ((), (), s32[]{:S(2)}) async-start(), calls=%async_computation.3 | async-start | bytes 1880064 | tf_op jit(solution)/shard_map/all_gather | solution.py:1085
  10.2 141.6 %all-gather.8.cloned.1.call-start = ((), (), s32[]{:S(2)}) async-start(), calls=%async_computation.4 | async-start | bytes 1253376 | tf_op jit(solution)/shard_map/all_gather | solution.py:1086
  11.8 193.3 %all-gather.10.cloned.1.call-start = ((), (), s32[]{:S(2)}) async-start(), calls=%async_computation.5 | async-start | bytes 10027008 | tf_op jit(solution)/shard_map/all_gather | solution.py:1087
  37.2 45.5 %copy-start.38 = (f32[768]{0:T(1024)}, f32[768]{0:T(1024)S(1)}, u32[]{:S(2)}) copy-start(f32[768]{0:T(1024)S(1)} %get-tuple-element.117) | copy-start | bytes 9220
  41.4 47.3 %copy-start.30 = (f32[1024]{0:T(1024)}, f32[1024]{0:T(1024)S(1)}, u32[]{:S(2)}) copy-start(f32[1024]{0:T(1024)S(1)} %broadcast_multiply_fusion.3) | copy-start | bytes 12292
  42.0 46.7 %copy-start.41 = (f32[1024]{0:T(1024)}, f32[1024]{0:T(1024)S(1)}, u32[]{:S(2)}) copy-start(f32[1024]{0:T(1024)S(1)} %add_rsqrt_fusion) | copy-start | bytes 12292
  144.1 7.5 %copy-start = (bf16[1,512,768]{2,1,0:T(8,128)(2,1)S(1)}, bf16[1,512,768]{2,1,0:T(8,128)(2,1)}, u32[]{:S(2)}) copy-start(bf16[1,512,768]{2,1,0:T(8,128)(2,1)} %param.14) | copy-start | bytes 2359300
  146.4 15.2 %all-to-all-start = ((bf16[2,512,384]{1,2,0:T(8,128)(2,1)}), bf16[2,512,384]{1,2,0:T(8,128)(2,1)S(1)}, u32[]{:S(2)}, u32[]{:S(2)}) async-start(bf16[2,512,384]{1,2,0:T(8,128)(2,1)} %copy.102), calls=%async_computation | async-start | bytes 1572864 | tf_op jit(solution)/shard_map/all_to_all | solution.py:1098
  151.7 199.1 %copy-start.26 = (f32[512]{0:T(512)}, f32[512]{0:T(512)S(1)}, u32[]{:S(2)}) copy-start(f32[512]{0:T(512)S(1)} %broadcast_multiply_fusion.5) | copy-start | bytes 6148
  164.0 52.7 %copy-start.4 = (f32[512,768]{1,0:T(8,128)}, f32[512,768]{1,0:T(8,128)S(1)}, u32[]{:S(2)}) copy-start(f32[512,768]{1,0:T(8,128)S(1)} %get-tuple-element.150) | copy-start | bytes 4718596
  224.2 15.0 %all-to-all-start.1 = ((bf16[512,2,384]{2,0,1:T(8,128)(2,1)}), bf16[512,2,384]{2,0,1:T(8,128)(2,1)S(1)}, u32[]{:S(2)}, u32[]{:S(2)}) async-start(bf16[512,2,384]{2,0,1:T(8,128)(2,1)} %bitcast.208), calls=%async_computation.1 | async-start | bytes 1572864 | tf_op jit(solution)/shard_map/all_to_all | solution.py:1120
  227.8 123.1 %reduce-scatter.2.cloned.1.call-start = ((), (), s32[]{:S(2)}) async-start(), calls=%async_computation.6 | async-start | bytes 2359296 | tf_op jit(solution)/shard_map/reduce_scatter | solution.py:1127
  228.2 122.7 %copy-start.28 = (f32[512]{0:T(512)}, f32[512]{0:T(512)S(1)}, u32[]{:S(2)}) copy-start(f32[512]{0:T(512)S(1)} %add_rsqrt_fusion.1) | copy-start | bytes 6148
  240.1 74.8 %copy-start.46 = (bf16[768,1152]{1,0:T(8,128)(2,1)S(1)}, bf16[768,1152]{1,0:T(8,128)(2,1)}, u32[]{:S(2)}) copy-start(bf16[768,1152]{1,0:T(8,128)(2,1)} %all-gather.6.cloned.1.call-done) | copy-start | bytes 5308420
  319.9 7.6 %copy-start.44 = (bf16[768]{0:T(1024)(128)(2,1)S(1)}, bf16[768]{0:T(1024)(128)(2,1)}, u32[]{:S(2)}) copy-start(bf16[768]{0:T(1024)(128)(2,1)} %get-tuple-element.113) | copy-start | bytes 4612
  319.9 7.8 %copy-start.10 = (bf16[2,512,384]{1,2,0:T(8,128)(2,1)S(1)}, bf16[2,512,384]{1,2,0:T(8,128)(2,1)}, u32[]{:S(2)}) copy-start(bf16[2,512,384]{1,2,0:T(8,128)(2,1)} %copy-done.9) | copy-start | bytes 2359300
  327.7 10.7 %slice-start = ((s8[9437184]{0:T(1024)(128)(4,1)}), s8[4194304]{0:T(1024)(128)(4,1)S(1)}, s32[]{:S(2)}) async-start(s8[9437184]{0:T(1024)(128)(4,1)} %bitcast.223), calls=%async_computation.8 | async-start | bytes 8388608
  327.7 10.7 %slice-start.3 = ((s8[6291456]{0:T(1024)(128)(4,1)}), s8[4194304]{0:T(1024)(128)(4,1)S(1)}, s32[]{:S(2)}) async-start(s8[6291456]{0:T(1024)(128)(4,1)} %bitcast.225), calls=%async_computation.11 | async-start | bytes 8388608
  329.6 8.8 %copy-start.5 = (f32[512,768]{1,0:T(8,128)S(1)}, f32[512,768]{1,0:T(8,128)}, u32[]{:S(2)}) copy-start(f32[512,768]{1,0:T(8,128)} %copy-done.4) | copy-start | bytes 4718596
  329.6 8.9 %slice-start.1 = ((s8[9437184]{0:T(1024)(128)(4,1)}), s8[4194304]{0:T(1024)(128)(4,1)S(1)}, s32[]{:S(2)}) async-start(s8[9437184]{0:T(1024)(128)(4,1)} %bitcast.223), calls=%async_computation.9 | async-start | bytes 8388608
  329.6 8.9 %slice-start.2 = ((s8[9437184]{0:T(1024)(128)(4,1)}), s8[1048576]{0:T(1024)(128)(4,1)S(1)}, s32[]{:S(2)}) async-start(s8[9437184]{0:T(1024)(128)(4,1)} %bitcast.223), calls=%async_computation.10 | async-start | bytes 2097152
  329.6 8.9 %slice-start.4 = ((s8[6291456]{0:T(1024)(128)(4,1)}), s8[2097152]{0:T(1024)(128)(4,1)S(1)}, s32[]{:S(2)}) async-start(s8[6291456]{0:T(1024)(128)(4,1)} %bitcast.225), calls=%async_computation.12 | async-start | bytes 4194304
  445.5 20.9 %copy-start.15 = (bf16[1,48,2304]{2,1,0:T(8,128)(2,1)S(1)}, bf16[1,48,2304]{2,1,0:T(8,128)(2,1)}, u32[]{:S(2)}) copy-start(bf16[1,48,2304]{2,1,0:T(8,128)(2,1)} %concatenate.73) | copy-start | bytes 663556
  (38 other events, 125.2 us)
Sparse Core Ops, SparseCore 0:
  9.6 29.8 all-gather.11
  42.2 40.3 all-gather.5
  85.5 36.9 all-gather.7
  124.6 80.4 all-gather.9
  320.0 23.3 reduce-scatter.1
